TPU v7x, 32 devices: a whole 2x2x4 slice. The times are simulated.
32 devices in a mesh: pair: 8 (over z, y), integral: 4 (over x, core).
Axes of the slice: x: 2, y: 2, z: 4, core: 2. Of those that a mesh axis runs over, the one named last changes fastest.
Arguments:
- occ_irrep: int32 [240], replicated, may hold values from 0 to 7
- amplitudes: bfloat16 [1920, 16384], P('pair', 'integral'), may hold values from -6 to 6
- ladder_ints: bfloat16 [16384, 16384], P('integral', 'pair'), may hold values from -0.046875 to 0.046875
- cycle_ints: bfloat16 [240, 128, 30720], P(None, 'integral', 'pair'), may hold values from -0.03125 to 0.03125
Outputs:
- residual: float32 [8, 240, 16384], P('integral', None, 'pair')
Inputs may be any that keep to these rules, and one draw needn't show every extreme that they name: `occ_irrep`: irrep labels of D2h, below 8.
All inputs are finite; a program needn't handle non-finite values.
Results may differ from a plain program's by a relative error of at most 0.0003.
Values may be sent and summed in bfloat16 or wider, within the bound.
A program may use at most 256 MiB of HBM per device.

v0:
```python
import jax
import jax.numpy as jnp
from jax import lax
from jax.sharding import PartitionSpec as P


def lookup_labels(indices, labels, occ_count):
    orbital = jnp.arange(occ_count, dtype=jnp.int32)
    return jnp.sum(jnp.where(indices[:, None] == orbital[None, :], labels[None, :], 0), axis=1)


def body(occ_irrep, amplitudes, ladder_ints, cycle_ints):
    rows_local = amplitudes.shape[0]
    occ_count, vir_part, cycle_cols = cycle_ints.shape
    vir_full = amplitudes.shape[1] // vir_part
    vir_local = cycle_cols // occ_count
    row_start = lax.axis_index("pair") * rows_local
    global_row = row_start + jnp.arange(rows_local, dtype=jnp.int32)
    label_first = lookup_labels(global_row // occ_count, occ_irrep, occ_count)
    label_second = lookup_labels(global_row % occ_count, occ_irrep, occ_count)
    allowed = label_first == label_second
    amp_sym = jnp.where(allowed[:, None], amplitudes, jnp.zeros((), amplitudes.dtype))
    gathered = lax.all_gather(amp_sym, "pair", axis=0, tiled=True)
    total_rows = gathered.shape[0]
    window = total_rows // occ_count
    ladder = jnp.dot(gathered, ladder_ints, preferred_element_type=jnp.float32)
    ladder = ladder.reshape(window, occ_count, vir_local * vir_full)
    cycle_term = jnp.einsum(
        "ixa,xn->ian",
        gathered.reshape(window, occ_count * vir_part, vir_full),
        cycle_ints.reshape(occ_count * vir_part, cycle_cols),
        preferred_element_type=jnp.float32,
    )
    cycle_term = cycle_term.reshape(window, vir_full, vir_local, occ_count)
    same_irrep = (occ_irrep[:window][:, None] == occ_irrep[None, :]).astype(jnp.float32)
    cycle_term = cycle_term * same_irrep[:, None, None, :]
    regrouped = lax.all_to_all(cycle_term, "pair", split_axis=1, concat_axis=2, tiled=True)
    rows_here = regrouped.shape[0]
    moved = jnp.transpose(regrouped, (0, 3, 1, 2)).reshape(
        rows_here, occ_count, vir_local * vir_full
    )
    combined = ladder + moved
    return lax.psum_scatter(combined, "integral", scatter_dimension=0, tiled=True)


def solution(mesh):
    placed = (P(), P("pair", "integral"), P("integral", "pair"), P(None, "integral", "pair"))
    return jax.shard_map(
        body, mesh=mesh, in_specs=placed, out_specs=P("integral", None, "pair"), check_vma=False
    )
```

profile of v0, /device:TPU:0, one launch (start us, length us, event | category | flops | bytes accessed | tf_op | source)
XLA Modules:
  0.0 879.8 jit_solution(2104946977953105363)
XLA Ops:
  6.5 0.0 all-gather.2.cloned.1.call-start
  6.6 0.9 select_reduce_fusion
  7.5 3.0 broadcast_select_fusion
  10.5 0.0 all-gather.2.cloned.1.call-update
  10.5 0.0 copy-start
  10.5 0.0 slice-start
  10.6 73.0 %copy.15 = bf16[3840,7680]{1,0:T(8,128)(2,1)} copy(bf16[3840,7680]{0,1:T(8,128)(2,1)} %bitcast.24) | data formatting | bytes 117964800 | tf_op jit(solution)/shard_map/ixa,xn->ian/dot_general | solution.py:28
  83.5 0.0 copy-done
  83.5 0.0 slice-done
  83.5 0.1 compare_convert_fusion
  83.6 144.6 %all-gather.2.cloned.1.call-done = bf16[1920,4096]{1,0:T(8,128)(2,1)} async-done(((bf16[240,4096]{1,0:T(8,128)(2,1)}), bf16[1920,4096]{1,0:T(8,128)(2,1)}) %all-gather.2.cloned.1.call-update) | async-done | bytes 15728656 | tf_op jit(solution)/shard_map/all_gather | solution.py:23
  228.2 24.2 %reshape.64 = bf16[8,7680,128,1]{2,1,0,3:T(8,128)(2,1)} reshape(bf16[1920,4096]{1,0:T(8,128)(2,1)} %all-gather.2.cloned.1.call-done) | data formatting | bytes 31457280 | tf_op jit(solution)/shard_map/reshape | solution.py:30
  252.4 71.2 %fusion.2 = f32[8,128,16,240]{1,3,2,0:T(8,128)} fusion(bf16[16,240,7680,1]{2,1,0,3:T(8,128)(2,1)} %bitcast.25, bf16[8,7680,128,1]{2,1,0,3:T(8,128)(2,1)} %reshape.64, f32[8,240]{1,0:T(8,128)S(1)} %compare_convert_fusion), kind=kOutput, calls=%fused_computation.2 | convolution fusion | flops 60401909760 | bytes 90447360 | tf_op jit(solution)/shard_map/ixa,xn->ian/dot_general | solution.py:28
  323.6 17.4 %copy.16 = f32[8,128,16,240]{3,2,0,1:T(8,128)} copy(f32[8,128,16,240]{1,3,2,0:T(8,128)} %fusion.2) | data formatting | bytes 31457280 | tf_op jit(solution)/shard_map/mul | solution.py:36
  340.9 5.7 all-to-all-start
  346.7 0.2 reduce-scatter.2.cloned.1.call-start
  346.9 40.7 %fusion.7 = f32[1920,2048]{1,0:T(8,128)} fusion(bf16[1920,4096]{1,0:T(8,128)(2,1)} %all-gather.2.cloned.1.call-done, bf16[4096,2048]{1,0:T(8,128)(2,1)} %param.6), kind=kOutput, calls=%fused_computation.14 | convolution fusion | flops 32212254720 | bytes 48234496 | tf_op jit(solution)/shard_map/dot_general | solution.py:26
  387.6 321.8 %all-to-all-done = f32[8,128,16,240]{3,2,0,1:T(8,128)} async-done(((f32[8,128,16,240]{3,2,0,1:T(8,128)}), f32[8,128,16,240]{3,2,0,1:T(8,128)}, u32[]{:S(2)}, u32[]{:S(2)}) %all-to-all-start) | async-done | bytes 15728672 | tf_op jit(solution)/shard_map/all_to_all | solution.py:37
  709.4 11.9 %copy.18 = f32[8,16,8,16,240]{4,3,2,1,0:T(8,128)} copy(f32[8,16,8,16,240]{4,3,0,1,2:T(8,128)} %bitcast.8) | data formatting | bytes 31457280 | tf_op jit(solution)/shard_map/all_to_all | solution.py:37
  721.3 16.3 %copy.19 = f32[8,240,2048]{2,1,0:T(8,128)} copy(f32[8,240,2048]{1,2,0:T(8,128)} %bitcast.23) | data formatting | bytes 31457280 | tf_op jit(solution)/shard_map/reshape | solution.py:39
  737.6 16.3 %add.36 = f32[8,240,2048]{2,1,0:T(8,128)} add(f32[8,240,2048]{2,1,0:T(8,128)} %bitcast.26, f32[8,240,2048]{2,1,0:T(8,128)} %copy.19) | non-fusion elementwise | flops 3932160 | bytes 47185920 | tf_op jit(solution)/shard_map/add | solution.py:42
  753.9 0.0 reduce-scatter.2.cloned.1.call-update
  754.0 119.0 %reduce-scatter.2.cloned.1.call-done = f32[2,240,2048]{2,1,0:T(8,128)} async-done(((f32[8,240,2048]{2,1,0:T(8,128)}), f32[2,240,2048]{2,1,0:T(8,128)}) %reduce-scatter.2.cloned.1.call-update) | async-done | bytes 3932176 | tf_op jit(solution)/shard_map/reduce_scatter | solution.py:43
  (2 shorter events, 0.0 us)
Async XLA Ops:
  6.5 221.7 %all-gather.2.cloned.1.call-start = ((), (), s32[]{:S(2)}) async-start(), calls=%async_computation.2 | async-start | bytes 17694720 | tf_op jit(solution)/shard_map/all_gather | solution.py:23
  10.5 73.0 %copy-start = (s32[240]{0:T(256)S(1)}, s32[240]{0:T(256)}, u32[]{:S(2)}) copy-start(s32[240]{0:T(256)} %param.4) | copy-start | bytes 2884
  10.5 73.0 %slice-start = ((s32[240]{0:T(256)}), s32[8]{0:T(128)S(1)}, s32[]{:S(2)}) async-start(s32[240]{0:T(256)} %param.4), calls=%async_computation.4 | async-start | bytes 1024 | tf_op jit(solution)/shard_map/slice | solution.py:35
  340.9 368.4 %all-to-all-start = ((f32[8,128,16,240]{3,2,0,1:T(8,128)}), f32[8,128,16,240]{3,2,0,1:T(8,128)}, u32[]{:S(2)}, u32[]{:S(2)}) async-start(f32[8,128,16,240]{3,2,0,1:T(8,128)} %copy.16), calls=%async_computation | async-start | bytes 33554432 | tf_op jit(solution)/shard_map/all_to_all | solution.py:37
  346.7 526.3 %reduce-scatter.2.cloned.1.call-start = ((), (), s32[]{:S(2)}) async-start(), calls=%async_computation.3 | async-start | bytes 19660800 | tf_op jit(solution)/shard_map/reduce_scatter | solution.py:43
Sparse Core Ops, SparseCore 0:
  10.7 217.4 all-gather.1
  754.1 118.8 reduce-scatter.1
where the time goes:
time: 883 us; the launch traced here: 880 us
  waiting for transfers between devices  585 us (66%)
  local copies, waits for them, and re-layouts  143 us (16%)
  matrix products  112 us (13%)
  other arithmetic  20.4 us (2%)
  between operations  13.4 us (2%)
    all_to_all x1, waiting for transfers between devices, body(): lax.all_to_all(cycle_term, 'pair', split_axis=1, concat_axis=2, tiled=True)  322 us
    all_gather x1, waiting for transfers between devices, body(): gathered = lax.all_gather(amp_sym, 'pair', axis=0, tiled=True)  145 us
    reduce_scatter x1, waiting for transfers between devices, body(): lax.psum_scatter(combined, 'integral', scatter_dimension=0, tiled=True)  119 us
    dot_general x1, local copies, waits for them, and re-layouts, body(): jnp.einsum('ixa,xn->ian', gathered.reshape(window, occ_count * vir_part,...  73 us
    dot_general x1, matrix products, body(): jnp.einsum('ixa,xn->ian', gathered.reshape(window, occ_count * vir_part,...  71.2 us
    dot_general x1, matrix products, body(): ladder = jnp.dot(gathered, ladder_ints, preferred_element_type=jnp.float32)  40.7 us
    reshape x1, local copies, waits for them, and re-layouts, body(): gathered.reshape(window, occ_count * vir_part, vir_full)  24.2 us
  transfers between devices with their start and end apart: 3, of which 3 were waited for; matrix products, arithmetic and copies ran while one was open for 13% of the time, Pallas kernels for 0%

commit v1 on v0

v1 whole, which is shorter than its diff:
```python
import jax
import jax.numpy as jnp
from jax import lax
from jax.sharding import PartitionSpec as P

STEPS = 32767.0


def lookup_labels(indices, labels, occ_count):
    orbital = jnp.arange(occ_count, dtype=jnp.int32)
    return jnp.sum(jnp.where(indices[:, None] == orbital[None, :], labels[None, :], 0), axis=1)


def encode(values, axis):
    largest = jnp.max(jnp.abs(values), axis=axis, keepdims=True)
    unit = largest * (1.0 / STEPS)
    inverse = jnp.where(largest > 0, STEPS / jnp.where(largest > 0, largest, 1.0), 0.0)
    return jnp.round(values * inverse).astype(jnp.int32).astype(jnp.int16), unit


def decode(codes, unit):
    return codes.astype(jnp.int32).astype(jnp.float32) * unit


def reduce_blocks(partial, axis_name, parts):
    me = lax.axis_index(axis_name)
    blocks = partial.reshape((parts, partial.shape[0] // parts) + partial.shape[1:])
    left, bit = parts, 1
    while left > 1:
        own = (me // bit) % 2
        halves = blocks.reshape((left // 2, 2) + blocks.shape[1:])
        give = lax.dynamic_index_in_dim(halves, 1 - own, 1, keepdims=False)
        keep = lax.dynamic_index_in_dim(halves, own, 1, keepdims=False)
        swap = [(d, d ^ bit) for d in range(parts)]
        if bit == 1:
            got = lax.ppermute(give, axis_name, swap)
        else:
            codes, unit = encode(give, 2)
            got = decode(lax.ppermute(codes, axis_name, swap), lax.ppermute(unit, axis_name, swap))
        blocks = keep + got
        left, bit = left // 2, bit * 2
    return blocks[0]


def body(occ_irrep, amplitudes, ladder_ints, cycle_ints, *, pairs, parts):
    rows_local = amplitudes.shape[0]
    occ, vir_part, cycle_cols = cycle_ints.shape
    vir = amplitudes.shape[1] // vir_part
    vir_local = cycle_cols // occ
    window = rows_local * pairs // occ
    row_start = lax.axis_index("pair") * rows_local
    global_row = row_start + jnp.arange(rows_local, dtype=jnp.int32)
    allowed = lookup_labels(global_row // occ, occ_irrep, occ) == lookup_labels(global_row % occ, occ_irrep, occ)
    amp_sym = jnp.where(allowed[:, None], amplitudes, jnp.zeros((), amplitudes.dtype))

    per_orbital = occ // rows_local
    cut = (rows_local + 31) // 32 * 16
    cuts = [(0, cut), (cut, rows_local)]
    ints = cycle_ints.reshape(per_orbital, rows_local, vir_part, cycle_cols)
    cols_half = cycle_cols // 2
    sums = [None, None]
    ladders = []
    for number, (first, last) in enumerate(cuts):
        size = last - first
        gathered = lax.all_gather(amp_sym[first:last], "pair", axis=0, tiled=True)
        if number:
            gathered, sums[0], sums[1], ladders[0] = lax.optimization_barrier((gathered, sums[0], sums[1], ladders[0]))
        left = gathered.reshape(window, per_orbital * size * vir_part, vir)
        right = ints[:, first:last].reshape(per_orbital * size * vir_part, cycle_cols)
        ladder = jnp.dot(gathered, ladder_ints, preferred_element_type=jnp.float32)
        ladder = ladder.reshape(window, per_orbital * size, vir_local * vir)
        for half in range(2):
            term = jnp.einsum(
                "ixa,xn->ian", left, right[:, half * cols_half:(half + 1) * cols_half],
                preferred_element_type=jnp.float32,
            )
            sums[half] = term if number == 0 else sums[half] + term
        ladder = reduce_blocks(ladder, "integral", parts)
        ladders.append(ladder.reshape(window // parts, per_orbital, size, vir_local * vir))

    mine = window // parts
    a_local = vir // pairs
    cycles = []
    for half in range(2):
        cycle = reduce_blocks(sums[half], "integral", parts)
        codes, unit = encode(cycle, 2)
        codes = lax.all_to_all(codes.reshape(mine, pairs, a_local, cols_half), "pair", 1, 1, tiled=True)
        unit = lax.all_to_all(unit.reshape(mine, pairs, a_local, 1), "pair", 1, 1, tiled=True)
        cycles.append(decode(codes, unit).reshape(mine, pairs, a_local, vir_local // 2, occ))
    ladder = jnp.concatenate(ladders, axis=2).reshape(mine, occ, vir_local * vir)

    cycle = jnp.stack(cycles, axis=2)
    cycle = jnp.transpose(cycle, (0, 5, 3, 1, 2, 4)).reshape(mine, occ, a_local * vir)
    own = lax.axis_index("integral") * mine + jnp.arange(mine, dtype=jnp.int32)
    same = lookup_labels(own, occ_irrep, occ)[:, None] == occ_irrep[None, :]
    return ladder + cycle * same.astype(jnp.float32)[:, :, None]


def solution(mesh):
    placed = (P(), P("pair", "integral"), P("integral", "pair"), P(None, "integral", "pair"))

    def local(*arrays):
        return body(*arrays, pairs=mesh.shape["pair"], parts=mesh.shape["integral"])

    return jax.shard_map(
        local, mesh=mesh, in_specs=placed, out_specs=P("integral", None, "pair"), check_vma=False
    )
```

time: 883 us -> 534 us (0.60)
  waiting for transfers between devices: 585 us -> 180 us
  other arithmetic: 20.4 us -> 45.6 us
  starting transfers between devices: 5.96 us -> 26.2 us
  matrix products: 112 us -> 130 us
  local copies, waits for them, and re-layouts: 143 us -> 130 us
    all_to_all x1 -> x4, waiting for transfers between devices: 322 us -> 26.1 us  [the longest x2 20.1 us: body(): lax.all_to_all(codes.reshape(mine, pairs, a_local, cols_half), 'pair', 1,...]
    reduce_scatter x1 -> x0, waiting for transfers between devices: 119 us -> none  [body(): lax.psum_scatter(combined, 'integral', scatter_dimension=0, tiled=True)]
    dot_general x1 -> x0, local copies, waits for them, and re-layouts: 73 us -> none  [body(): jnp.einsum('ixa,xn->ian', gathered.reshape(window, occ_count * vir_part,...]
    slice x2 -> x4, local copies, waits for them, and re-layouts: 0.01 us -> 43.7 us  [the longest x2 41.6 us: body(): ints[:, first:last].reshape(per_orbital * size * vir_part, cycle_cols)]
    ppermute x0 -> x12, waiting for transfers between devices: none -> 26.8 us  [the longest x4 26.8 us: reduce_blocks(): lax.ppermute(unit, axis_name, swap)]
    dynamic_slice x0 -> x5, local copies, waits for them, and re-layouts: none -> 26.8 us  [the longest x4 21.5 us: reduce_blocks(): keep = lax.dynamic_index_in_dim(halves, own, 1, keepdims=False)]
    all_gather x1 -> x2, waiting for transfers between devices: 145 us -> 127 us  [body(): gathered = lax.all_gather(amp_sym[first:last], 'pair', axis=0, tiled=True)]
    dot_general x1 -> x4, matrix products: 71.2 us -> 88.8 us  [body(): jnp.einsum('ixa,xn->ian', left, right[:, half * cols_half:(half + 1) * co...]
  transfers between devices with their start and end apart: 3 -> 18, of which waited for: 3 -> 7; matrix products, arithmetic and copies ran while one was open for 13% -> 47% of each run, Pallas kernels for 0% -> 0%
where the time goes in v1:
time: 534 us; the launch traced here: 525 us
  waiting for transfers between devices  180 us (34%)
  local copies, waits for them, and re-layouts  130 us (24%)
  matrix products  130 us (24%)
  other arithmetic  45.6 us (9%)
  starting transfers between devices  26.2 us (5%)
  between operations  14.2 us (3%)
    all_gather x2, waiting for transfers between devices, body(): gathered = lax.all_gather(amp_sym[first:last], 'pair', axis=0, tiled=True)  127 us
    dot_general x4, matrix products, body(): jnp.einsum('ixa,xn->ian', left, right[:, half * cols_half:(half + 1) * co...  88.8 us
    slice x2, local copies, waits for them, and re-layouts, body(): ints[:, first:last].reshape(per_orbital * size * vir_part, cycle_cols)  41.6 us
    dot_general x2, matrix products, body(): ladder = jnp.dot(gathered, ladder_ints, preferred_element_type=jnp.float32)  40.7 us
    ppermute x4, waiting for transfers between devices, reduce_blocks(): lax.ppermute(unit, axis_name, swap)  26.8 us
    reshape x2, local copies, waits for them, and re-layouts, body(): left = gathered.reshape(window, per_orbital * size * vir_part, vir)  25.4 us
    dynamic_slice x4, local copies, waits for them, and re-layouts, reduce_blocks(): keep = lax.dynamic_index_in_dim(halves, own, 1, keepdims=False)  21.5 us
    all_to_all x2, waiting for transfers between devices, body(): lax.all_to_all(codes.reshape(mine, pairs, a_local, cols_half), 'pair', 1,...  20.1 us
  transfers between devices with their start and end apart: 18, of which 7 were waited for; matrix products, arithmetic and copies ran while one was open for 47% of the time, Pallas kernels for 0%

profile of v1, /device:TPU:0, one launch (start us, length us, event | category | flops | bytes accessed | tf_op | source)
XLA Modules:
  0.0 525.4 jit_solution(13063615963914684321)
XLA Ops:
  11.5 126.6 %all-gather.5.cloned.1.call-done = bf16[1024,4096]{1,0:T(8,128)(2,1)} async-done(((bf16[128,4096]{1,0:T(8,128)(2,1)}), bf16[1024,4096]{1,0:T(8,128)(2,1)}) %all-gather.5.cloned.1.call-update) | async-done | bytes 8388624 | tf_op jit(solution)/shard_map/all_gather | solution.py:65
  138.1 21.4 %fusion.12 = f32[1024,2048]{1,0:T(8,128)S(1)} fusion(bf16[1024,4096]{1,0:T(8,128)(2,1)} %all-gather.5.cloned.1.call-done, bf16[4096,2048]{1,0:T(8,128)(2,1)} %param.6), kind=kOutput, calls=%fused_computation.76 | convolution fusion | flops 17179869184 | bytes 33554432 | tf_op jit(solution)/shard_map/dot_general | solution.py:70
  159.5 3.9 constant_dynamic-slice_fusion.2
  163.4 5.3 %copy.52 = f32[2,1,2,128,2048]{3,4,2,0,1:T(8,128)} copy(f32[2,1,2,128,2048]{4,3,2,1,0:T(8,128)} %get-tuple-element.20) | data formatting | bytes 8388608 | tf_op jit(solution)/shard_map/jit(dynamic_index_in_dim)/dynamic_slice | solution.py:32
  168.8 22.5 %slice.34 = bf16[1,128,32,3840]{3,2,1,0:T(8,128)(2,1)} slice(bf16[1,240,32,3840]{3,2,1,0:T(8,128)(2,1)} %bitcast.85), slice={[0:1], [0:128], [0:32], [0:3840]} | slice | bytes 62914560 | tf_op jit(solution)/shard_map/slice | solution.py:69
  191.3 19.1 %slice.37 = bf16[1,112,32,3840]{3,2,1,0:T(8,128)(2,1)} slice(bf16[1,240,32,3840]{3,2,1,0:T(8,128)(2,1)} %bitcast.86), slice={[0:1], [128:240], [0:32], [0:3840]} | slice | bytes 55050240 | tf_op jit(solution)/shard_map/slice | solution.py:69
  210.4 5.3 %copy.51 = f32[2,1,2,128,2048]{3,4,2,0,1:T(8,128)} copy(f32[2,1,2,128,2048]{4,3,2,1,0:T(8,128)} %get-tuple-element.19) | data formatting | bytes 8388608 | tf_op jit(solution)/shard_map/jit(dynamic_index_in_dim)/dynamic_slice | solution.py:33
  215.7 13.5 %reshape.285 = bf16[8,4096,128]{2,1,0:T(8,128)(2,1)} reshape(bf16[1024,4096]{1,0:T(8,128)(2,1)} %all-gather.5.cloned.1.call-done) | data formatting | bytes 16777216 | tf_op jit(solution)/shard_map/reshape | solution.py:68
  229.2 24.1 %fusion = f32[8,128,1920]{2,1,0:T(8,128)} fusion(bf16[8,4096,128]{2,1,0:T(8,128)(2,1)} %reshape.285, bf16[4096,3840]{1,0:T(8,128)(2,1)} %bitcast.87), kind=kOutput, calls=%fused_computation.1 | convolution fusion | flops 16106127360 | bytes 31981568 | tf_op jit(solution)/shard_map/ixa,xn->ian/dot_general | solution.py:73
  253.4 2.9 bitcast_add_fusion.1
  259.8 22.0 %fusion.1 = f32[8,128,1920]{2,1,0:T(8,128)} fusion(bf16[8,4096,128]{2,1,0:T(8,128)(2,1)S(1)} %copy-done.4, bf16[4096,3840]{1,0:T(8,128)(2,1)} %bitcast.88), kind=kOutput, calls=%fused_computation.3 | convolution fusion | flops 16106127360 | bytes 31981568 | tf_op jit(solution)/shard_map/ixa,xn->ian/dot_general | solution.py:73
  283.8 11.9 %reshape.289 = bf16[8,3584,128]{2,1,0:T(8,128)(2,1)} reshape(bf16[896,4096]{1,0:T(8,128)(2,1)} %all-gather.3.cloned.1.call-done) | data formatting | bytes 14680064 | tf_op jit(solution)/shard_map/reshape | solution.py:68
  295.7 21.0 %fusion.5 = f32[8,128,1920]{2,1,0:T(8,128)S(1)} fusion(f32[8,128,1920]{2,1,0:T(8,128)} %fusion.1, bf16[8,3584,128]{2,1,0:T(8,128)(2,1)} %reshape.289, bf16[3584,3840]{1,0:T(8,128)(2,1)} %bitcast.89), kind=kOutput, calls=%fused_computation.18 | convolution fusion | flops 14094827520 | bytes 36831232 | tf_op jit(solution)/shard_map/ixa,xn->ian/dot_general | solution.py:73
  319.0 21.7 %fusion.6 = f32[8,128,1920]{2,1,0:T(8,128)S(1)} fusion(f32[8,128,1920]{2,1,0:T(8,128)} %fusion, bf16[8,3584,128]{2,1,0:T(8,128)(2,1)} %reshape.289, bf16[3584,3840]{1,0:T(8,128)(2,1)} %bitcast.90), kind=kOutput, calls=%fused_computation.19 | convolution fusion | flops 14094827520 | bytes 36831232 | tf_op jit(solution)/shard_map/ixa,xn->ian/dot_general | solution.py:73
  343.0 19.3 %fusion.13 = f32[896,2048]{1,0:T(8,128)} fusion(bf16[896,4096]{1,0:T(8,128)(2,1)S(1)} %bitcast.99, bf16[4096,2048]{1,0:T(8,128)(2,1)} %param.6), kind=kOutput, calls=%fused_computation.77 | convolution fusion | flops 15032385536 | bytes 31457280 | tf_op jit(solution)/shard_map/dot_general | solution.py:70
  362.3 7.1 %constant_dynamic-slice_fusion = (f32[2,1,2,112,2048]{4,3,2,1,0:T(8,128)}, f32[2,2,112,2048]{3,2,1,0:T(8,128)}) fusion(f32[2,2,2,112,2048]{4,3,2,1,0:T(8,128)} %bitcast.100, s32[]{:T(128)S(6)} %select_n.203, s32[]{:T(128)S(6)} %select_n.204), kind=kLoop, calls=%fused_computation.62 | loop fusion | bytes 14680072 | tf_op jit(solution)/shard_map/jit(dynamic_index_in_dim)/dynamic_slice | solution.py:33
  383.4 5.1 copy.53
  388.5 5.2 copy.54
  394.3 25.5 %collective-permute-done.8 = f32[1,2,1,1920]{3,1,2,0:T(2,128)S(1)} collective-permute-done((f32[1,2,1,1920]{3,1,2,0:T(2,128)S(1)}, f32[1,2,1,1920]{3,1,2,0:T(2,128)S(1)}, u32[]{:S(2)}, u32[]{:S(2)}) %collective-permute-start.8) | collective-permute-done | bytes 15392 | tf_op jit(solution)/shard_map/ppermute | solution.py:39
  419.9 3.6 abs_reduce_fusion.4
  424.2 3.3 all-to-all-start.1
  427.6 3.4 abs_reduce_fusion.2
  434.0 3.6 all-to-all-start.3
  440.3 3.7 all-to-all-done.3
  444.1 4.2 all-to-all-start
  448.3 3.9 bitcast_add_fusion
  461.0 10.1 %all-to-all-done = s16[2,8,16,1920]{3,2,0,1:T(8,128)(2,1)} async-done(((s16[2,8,16,1920]{3,2,0,1:T(8,128)(2,1)}), s16[2,8,16,1920]{3,2,0,1:T(8,128)(2,1)}, u32[]{:S(2)}, u32[]{:S(2)}) %all-to-all-start) | async-done | bytes 983072 | tf_op jit(solution)/shard_map/all_to_all | solution.py:87
  471.1 4.5 all-to-all-start.2
  485.4 3.8 reshape.296
  489.2 10.0 %all-to-all-done.2 = s16[2,8,16,1920]{3,2,0,1:T(8,128)(2,1)} async-done(((s16[2,8,16,1920]{3,2,0,1:T(8,128)(2,1)}), s16[2,8,16,1920]{3,2,0,1:T(8,128)(2,1)}, u32[]{:S(2)}, u32[]{:S(2)}) %all-to-all-start.2) | async-done | bytes 983072 | tf_op jit(solution)/shard_map/all_to_all | solution.py:87
  502.0 3.8 reshape.297
  512.8 5.3 %copy.66 = f32[2,240,2048]{2,1,0:T(8,128)} copy(f32[2,240,2048]{1,2,0:T(8,128)} %fusion.4) | data formatting | bytes 7864320 | tf_op jit(solution)/shard_map/add | solution.py:96
  (96 shorter events, 64.4 us)
Async XLA Ops:
  6.5 131.6 %all-gather.5.cloned.1.call-start = ((), (), s32[]{:S(2)}) async-start(), calls=%async_computation.5 | async-start | bytes 9437184 | tf_op jit(solution)/shard_map/all_gather | solution.py:65
  10.3 273.5 %all-gather.3.cloned.1.call-start = ((), (), s32[]{:S(2)}) async-start(), calls=%async_computation.4 | async-start | bytes 8257536 | tf_op jit(solution)/shard_map/all_gather | solution.py:65
  168.8 84.6 %collective-permute-start = (f32[2,2,128,2048]{2,3,1,0:T(8,128)}, f32[2,2,128,2048]{2,3,1,0:T(8,128)}, u32[]{:S(2)}, u32[]{:S(2)}) collective-permute-start(f32[2,2,128,2048]{2,3,1,0:T(8,128)} %bitcast.101), channel_id=1, source_target_pairs={{0,1},{1,0},{2,3},{3,2},{4,5},{5,4},{6,7},{7,6},{8,9},{9,8},{10,11... | collective-permute-start | bytes 12582920 | tf_op jit(solution)/shard_map/ppermute | solution.py:36
  229.2 24.2 %copy-start.3 = (f32[2,1,2,128,2048]{3,4,2,0,1:T(8,128)S(1)}, f32[2,1,2,128,2048]{3,4,2,0,1:T(8,128)}, u32[]{:S(2)}) copy-start(f32[2,1,2,128,2048]{3,4,2,0,1:T(8,128)} %copy.51) | copy-start | bytes 12582916
  253.3 6.4 %copy-start.4 = (bf16[8,4096,128]{2,1,0:T(8,128)(2,1)S(1)}, bf16[8,4096,128]{2,1,0:T(8,128)(2,1)}, u32[]{:S(2)}) copy-start(bf16[8,4096,128]{2,1,0:T(8,128)(2,1)} %reshape.285) | copy-start | bytes 25165828
  257.7 25.4 %collective-permute-start.1 = (s16[1,2,128,2048]{2,3,1,0:T(8,128)(2,1)S(1)}, s16[1,2,128,2048]{2,3,1,0:T(8,128)(2,1)S(1)}, u32[]{:S(2)}, u32[]{:S(2)}) collective-permute-start(s16[1,2,128,2048]{2,3,1,0:T(8,128)(2,1)S(1)} %convert_convert_fusion.1), channel_id=1, source_target_pairs={{0,2},{1,3},{2,0},{3,1},{4,6},{5,7},{6,4},{7,5},{8,10},{9,11},{10,... | collective-permute-start | bytes 3145736 | tf_op jit(solution)/shard_map/ppermute | solution.py:39
  258.7 24.3 %collective-permute-start.2 = (f32[1,2,1,2048]{3,1,2,0:T(2,128)S(1)}, f32[1,2,1,2048]{3,1,2,0:T(2,128)S(1)}, u32[]{:S(2)}, u32[]{:S(2)}) collective-permute-start(f32[1,2,1,2048]{3,1,2,0:T(2,128)S(1)} %get-tuple-element.25), channel_id=1, source_target_pairs={{0,2},{1,3},{2,0},{3,1},{4,6},{5,7},{6,4},{7,5},{8,10},{9,11},{10,... | collective-permute-start | bytes 49160 | tf_op jit(solution)/shard_map/ppermute | solution.py:39
  316.8 26.2 %slice-start = ((s8[7340032]{0:T(1024)(128)(4,1)}), s8[4194304]{0:T(1024)(128)(4,1)S(1)}, s32[]{:S(2)}) async-start(s8[7340032]{0:T(1024)(128)(4,1)} %bitcast.98), calls=%async_computation.6 | async-start | bytes 8388608
  319.0 24.0 %slice-start.1 = ((s8[7340032]{0:T(1024)(128)(4,1)}), s8[3145728]{0:T(1024)(128)(4,1)S(1)}, s32[]{:S(2)}) async-start(s8[7340032]{0:T(1024)(128)(4,1)} %bitcast.98), calls=%async_computation.7 | async-start | bytes 6291456
  319.0 50.8 %collective-permute-start.6 = (f32[2,2,128,1920]{3,2,1,0:T(8,128)}, f32[2,2,128,1920]{3,2,1,0:T(8,128)}, u32[]{:S(2)}, u32[]{:S(2)}) collective-permute-start(f32[2,2,128,1920]{3,2,1,0:T(8,128)} %dynamic-slice_bitcast_fusion.1), channel_id=1, source_target_pairs={{0,1},{1,0},{2,3},{3,2},{4,5},{5,4},{6,7},{7,6},{8,9},{9,8},{10,11... | collective-permute-start | bytes 11796488 | tf_op jit(solution)/shard_map/ppermute | solution.py:36
  342.9 32.8 %collective-permute-start.9 = (f32[2,2,128,1920]{3,2,1,0:T(8,128)}, f32[2,2,128,1920]{3,2,1,0:T(8,128)}, u32[]{:S(2)}, u32[]{:S(2)}) collective-permute-start(f32[2,2,128,1920]{3,2,1,0:T(8,128)} %dynamic-slice_bitcast_fusion), channel_id=1, source_target_pairs={{0,1},{1,0},{2,3},{3,2},{4,5},{5,4},{6,7},{7,6},{8,9},{9,8},{10,11... | collective-permute-start | bytes 11796488 | tf_op jit(solution)/shard_map/ppermute | solution.py:36
  369.4 19.1 %collective-permute-start.3 = (f32[2,2,112,2048]{3,2,1,0:T(8,128)}, f32[2,2,112,2048]{3,2,1,0:T(8,128)}, u32[]{:S(2)}, u32[]{:S(2)}) collective-permute-start(f32[2,2,112,2048]{3,2,1,0:T(8,128)} %get-tuple-element.22), channel_id=1, source_target_pairs={{0,1},{1,0},{2,3},{3,2},{4,5},{5,4},{6,7},{7,6},{8,9},{9,8},{10,11... | collective-permute-start | bytes 11010056 | tf_op jit(solution)/shard_map/ppermute | solution.py:36
  372.3 3.4 copy-start.2
  373.9 45.9 %collective-permute-start.7 = (s16[1,2,128,1920]{3,2,1,0:T(8,128)(2,1)}, s16[1,2,128,1920]{3,2,1,0:T(8,128)(2,1)}, u32[]{:S(2)}, u32[]{:S(2)}) collective-permute-start(s16[1,2,128,1920]{3,2,1,0:T(8,128)(2,1)} %convert_convert_fusion.5), channel_id=1, source_target_pairs={{0,2},{1,3},{2,0},{3,1},{4,6},{5,7},{6,4},{7,5},{8,10},{9,11},{10,... | collective-permute-start | bytes 2949128 | tf_op jit(solution)/shard_map/ppermute | solution.py:39
  378.2 1.9 copy-start.1
  381.3 46.2 %collective-permute-start.10 = (s16[1,2,128,1920]{3,2,1,0:T(8,128)(2,1)}, s16[1,2,128,1920]{3,2,1,0:T(8,128)(2,1)S(1)}, u32[]{:S(2)}, u32[]{:S(2)}) collective-permute-start(s16[1,2,128,1920]{3,2,1,0:T(8,128)(2,1)} %convert_convert_fusion.3), channel_id=1, source_target_pairs={{0,2},{1,3},{2,0},{3,1},{4,6},{5,7},{6,4},{7,5},{8,10},{9,11},{10,... | collective-permute-start | bytes 2949128 | tf_op jit(solution)/shard_map/ppermute | solution.py:39
  381.9 37.9 %collective-permute-start.8 = (f32[1,2,1,1920]{3,1,2,0:T(2,128)S(1)}, f32[1,2,1,1920]{3,1,2,0:T(2,128)S(1)}, u32[]{:S(2)}, u32[]{:S(2)}) collective-permute-start(f32[1,2,1,1920]{3,1,2,0:T(2,128)S(1)} %get-tuple-element.28), channel_id=1, source_target_pairs={{0,2},{1,3},{2,0},{3,1},{4,6},{5,7},{6,4},{7,5},{8,10},{9,11},{10,... | collective-permute-start | bytes 46088 | tf_op jit(solution)/shard_map/ppermute | solution.py:39
  393.7 33.8 %collective-permute-start.11 = (f32[1,2,1,1920]{3,1,2,0:T(2,128)S(1)}, f32[1,2,1,1920]{3,1,2,0:T(2,128)S(1)}, u32[]{:S(2)}, u32[]{:S(2)}) collective-permute-start(f32[1,2,1,1920]{3,1,2,0:T(2,128)S(1)} %get-tuple-element.30), channel_id=1, source_target_pairs={{0,2},{1,3},{2,0},{3,1},{4,6},{5,7},{6,4},{7,5},{8,10},{9,11},{10,... | collective-permute-start | bytes 46088 | tf_op jit(solution)/shard_map/ppermute | solution.py:39
  424.2 9.7 %all-to-all-start.1 = ((f32[2,8,16,1]{2,0,3,1:T(2,128)}), f32[2,8,16,1]{2,0,3,1:T(2,128)S(1)}, u32[]{:S(2)}, u32[]{:S(2)}) async-start(f32[2,8,16,1]{2,0,3,1:T(2,128)} %copy.59), calls=%async_computation.1 | async-start | bytes 16384 | tf_op jit(solution)/shard_map/all_to_all | solution.py:88
  434.0 10.1 %all-to-all-start.3 = ((f32[2,8,16,1]{2,0,3,1:T(2,128)}), f32[2,8,16,1]{2,0,3,1:T(2,128)S(1)}, u32[]{:S(2)}, u32[]{:S(2)}) async-start(f32[2,8,16,1]{2,0,3,1:T(2,128)} %copy.63), calls=%async_computation.3 | async-start | bytes 16384 | tf_op jit(solution)/shard_map/all_to_all | solution.py:88
  444.1 27.1 %all-to-all-start = ((s16[2,8,16,1920]{3,2,0,1:T(8,128)(2,1)}), s16[2,8,16,1920]{3,2,0,1:T(8,128)(2,1)}, u32[]{:S(2)}, u32[]{:S(2)}) async-start(s16[2,8,16,1920]{3,2,0,1:T(8,128)(2,1)} %copy.58), calls=%async_computation | async-start | bytes 1966080 | tf_op jit(solution)/shard_map/all_to_all | solution.py:87
  452.2 1.9 copy-start
  456.4 19.3 %copy-start.6 = (s32[240]{0:T(256)S(1)}, s32[240]{0:T(256)}, u32[]{:S(2)}) copy-start(s32[240]{0:T(256)} %param.4) | copy-start | bytes 2884
  456.4 21.3 %collective-permute-start.4 = (s16[1,2,112,2048]{3,2,1,0:T(8,128)(2,1)}, s16[1,2,112,2048]{3,2,1,0:T(8,128)(2,1)}, u32[]{:S(2)}, u32[]{:S(2)}) collective-permute-start(s16[1,2,112,2048]{3,2,1,0:T(8,128)(2,1)} %copy.55), channel_id=1, source_target_pairs={{0,2},{1,3},{2,0},{3,1},{4,6},{5,7},{6,4},{7,5},{8,10},{9,11},{10,... | collective-permute-start | bytes 2752520 | tf_op jit(solution)/shard_map/ppermute | solution.py:39
  471.1 28.1 %all-to-all-start.2 = ((s16[2,8,16,1920]{3,2,0,1:T(8,128)(2,1)}), s16[2,8,16,1920]{3,2,0,1:T(8,128)(2,1)}, u32[]{:S(2)}, u32[]{:S(2)}) async-start(s16[2,8,16,1920]{3,2,0,1:T(8,128)(2,1)} %copy.62), calls=%async_computation.2 | async-start | bytes 1966080 | tf_op jit(solution)/shard_map/all_to_all | solution.py:87
  475.8 3.8 collective-permute-start.5
  508.4 1.6 copy-start.5
Sparse Core Ops, SparseCore 0:
  10.4 127.6 all-gather.4
  140.3 110.1 all-gather.2
